TPU v7x, 32 devices: a whole 2x2x4 slice. The times are simulated.
32 devices in a mesh: section: 2 (over y), tensor: 2 (over x), dp: 8 (over z, core).
Axes of the slice: x: 2, y: 2, z: 4, core: 2. Of those that a mesh axis runs over, the one named last changes fastest.
Arguments:
- query_rows: bfloat16 [8192, 8192], P(('section', 'dp'), 'tensor'), may hold values from -108 to 108
- key_rows: bfloat16 [8192, 1024], P(('section', 'dp'), 'tensor'), may hold values from -4.5 to 4.5
- rows_of_values: bfloat16 [8192, 1024], P(('section', 'dp'), 'tensor'), may hold values from -6 to 6
- cached_key_rows: bfloat16 [1024, 16, 1024], P('dp', None, 'tensor'), may hold values from -6 to 6
- cached_value_rows: bfloat16 [1024, 16, 1024], P('dp', None, 'tensor'), may hold values from -6 to 6
- cache_lengths: int32 [1024], P('dp'), may hold values from 1 to 16, 8192 in all
- prompt_lengths: int32 [4], replicated, may hold values from 1 to 2048, 4096 in all
- owners: int32 [4], replicated, may hold values from 0 to 7, as said below
- out_weight: bfloat16 [8192, 5120], P('tensor'), may hold values from -0.25 to 0.25
Outputs:
- layer_rows: bfloat16 [8192, 5120], P(('section', 'dp'), 'tensor')
Inputs may be any that keep to these rules, and one draw needn't show every extreme that they name: `cache_lengths`: the cached positions of a request number 1 to 16; the largest is 16. `prompt_lengths`: the prompt lengths sum to 4096; the longest is 2048. The owners of the new requests are distinct.
All inputs are finite; a program needn't handle non-finite values. No bound on the sum of `cache_lengths` on one device may be relied on, other than what follows from the above.
Results may differ from a plain program's by a relative error of at most 0.013.
Values may be sent and summed in bfloat16 or wider, within the bound.
A program may use at most 256 MiB of HBM per device.

v0:
```python
import jax
import jax.numpy as jnp
from jax import lax
from jax.sharding import PartitionSpec as P

HEAD_SIZE = 128
STEPS = 4
MAXLEN = 2048


masked_score = -1e30


def shifted(array, axis, by):
    count = lax.axis_size(axis)
    pairs = [(i, i + by) for i in range(count) if 0 <= i + by < count]
    return lax.ppermute(array, axis, pairs)


def attend_rows(queries, key_block, value_block, allowed):
    row_count = queries.shape[0]
    key_count = key_block.shape[0]
    heads_kv = key_block.shape[1] // HEAD_SIZE
    group_size = queries.shape[1] // key_block.shape[1]
    query_heads = queries.reshape(row_count, heads_kv, group_size, HEAD_SIZE)
    query_groups = jnp.moveaxis(query_heads, 2, 0)
    key_heads = key_block.reshape(key_count, heads_kv, HEAD_SIZE)
    value_heads = value_block.reshape(key_count, heads_kv, HEAD_SIZE)

    def one_group(query_group):
        scores = jnp.einsum(
            "rkd,wkd->krw", query_group, key_heads, preferred_element_type=jnp.float32
        ) * HEAD_SIZE ** (-0.5)
        scores = jnp.where(allowed[None], scores, masked_score)
        row_max = jnp.max(scores, axis=-1, keepdims=True)
        exponent = jnp.exp(scores - row_max)
        weights = (exponent / jnp.sum(exponent, axis=-1, keepdims=True)).astype(jnp.bfloat16)
        return jnp.einsum(
            "krw,wkd->rkd", weights, value_heads, preferred_element_type=jnp.float32
        ).astype(jnp.bfloat16)

    mixed = jnp.moveaxis(lax.map(one_group, query_groups), 0, 2)
    return mixed.reshape(row_count, -1)


def attend_slots(queries, key_block, value_block, lower, upper, context):
    step_count = queries.shape[1]
    key_count = key_block.shape[1]
    position = jnp.arange(key_count, dtype=jnp.int32)
    step_index = jnp.arange(step_count, dtype=jnp.int32)
    inside = (
        (position[None, None, :] >= lower[:, None, None])
        & (position[None, None, :] < upper[:, None, None])
        & (position[None, None, :] < context)
    )
    own_steps = (position[None, None, :] >= context) & (
        position[None, None, :] - context <= step_index[None, :, None]
    )
    return jax.vmap(attend_rows)(queries, key_block, value_block, inside | own_steps)


def on_device(
    query_rows,
    key_rows,
    rows_of_values,
    cached_key_rows,
    cached_value_rows,
    cache_lengths,
    prompt_lengths,
    owners,
    out_weight,
):
    row_count = query_rows.shape[0]
    prompt_total = row_count * lax.axis_size("dp")
    key_window = MAXLEN + row_count
    owner_index = lax.axis_index("dp")
    first_section = lax.axis_index("section") == 0
    first_row = owner_index * row_count
    starts = jnp.cumsum(prompt_lengths) - prompt_lengths
    is_owner = (owners == owner_index).astype(jnp.int32)
    has_new = jnp.sum(is_owner) > 0
    new_start = jnp.sum(is_owner * starts)
    new_length = jnp.sum(is_owner * prompt_lengths)
    slice_start = jnp.clip(new_start, 0, prompt_total - MAXLEN)
    whole_keys, whole_values = (
        lax.all_gather(key_rows, "dp", axis=0, tiled=True),
        lax.all_gather(rows_of_values, "dp", axis=0, tiled=True),
    )
    picked_keys = lax.dynamic_slice_in_dim(whole_keys, slice_start, MAXLEN, 0)
    picked_values = lax.dynamic_slice_in_dim(whole_values, slice_start, MAXLEN, 0)
    context_keys, context_values = shifted((picked_keys, picked_values), "section", 1)
    window_start = jnp.clip(first_row - MAXLEN, 0, prompt_total - key_window)
    key_block = lax.dynamic_slice_in_dim(whole_keys, window_start, key_window, 0)
    value_block = lax.dynamic_slice_in_dim(whole_values, window_start, key_window, 0)

    def prefill_branch():
        query_pos = first_row + jnp.arange(row_count, dtype=jnp.int32)
        query_start = jnp.max(
            jnp.where(starts[None, :] <= query_pos[:, None], starts[None, :], 0), axis=1
        )
        key_pos = window_start + jnp.arange(key_window, dtype=jnp.int32)
        allowed = (key_pos[None, :] >= query_start[:, None]) & (
            key_pos[None, :] <= query_pos[:, None]
        )
        return attend_rows(query_rows, key_block, value_block, allowed)

    def decode_branch():
        slot_count = row_count // STEPS
        cache_size = cached_key_rows.shape[1]
        step_queries = query_rows.reshape(slot_count, STEPS, -1)
        step_keys = key_rows.reshape(slot_count, STEPS, -1)
        step_values = rows_of_values.reshape(slot_count, STEPS, -1)
        offset = new_start - slice_start
        lower = jnp.where(has_new, offset, MAXLEN)
        upper = jnp.where(has_new, offset + new_length, MAXLEN + cache_lengths[0])
        fresh = attend_slots(
            step_queries[:1],
            jnp.concatenate([context_keys, cached_key_rows[0], step_keys[0]], 0)[None],
            jnp.concatenate([context_values, cached_value_rows[0], step_values[0]], 0)[None],
            lower[None],
            upper[None],
            MAXLEN + cache_size,
        )
        older = attend_slots(
            step_queries[1:],
            jnp.concatenate([cached_key_rows[1:], step_keys[1:]], 1),
            jnp.concatenate([cached_value_rows[1:], step_values[1:]], 1),
            jnp.zeros_like(cache_lengths[1:]),
            cache_lengths[1:],
            cache_size,
        )
        return jnp.concatenate([fresh, older], 0).reshape(row_count, -1)

    mixed = lax.cond(first_section, prefill_branch, decode_branch)
    columns = out_weight.shape[1] // lax.axis_size("tensor")
    summed = lax.psum(
        jnp.dot(mixed, out_weight, preferred_element_type=jnp.float32).astype(jnp.bfloat16),
        "tensor",
    ).astype(jnp.float32)
    return lax.dynamic_slice_in_dim(summed, lax.axis_index("tensor") * columns, columns, 1).astype(
        jnp.bfloat16
    )


def solution(mesh):
    placed = (
        P(("section", "dp"), "tensor"),
        P(("section", "dp"), "tensor"),
        P(("section", "dp"), "tensor"),
        P("dp", None, "tensor"),
        P("dp", None, "tensor"),
        P("dp"),
        P(),
        P(),
        P("tensor", None),
    )
    return jax.shard_map(
        on_device,
        mesh=mesh,
        in_specs=placed,
        out_specs=P(("section", "dp"), "tensor"),
        check_vma=False,
    )
```

profile of v0, /device:TPU:11, one launch (start us, length us, event | category | flops | bytes accessed | tf_op | source)
XLA Modules:
  0.0 576.3 jit_solution(3943980946888748654)
XLA Ops:
  6.5 0.0 all-gather.3.cloned.1.call-start
  6.5 2.0 copy.86
  8.6 0.0 all-gather.3.cloned.1.call-update
  8.6 0.0 all-gather.5.cloned.1.call-start
  8.7 2.0 copy.87
  10.7 0.0 all-gather.5.cloned.1.call-update
  10.7 0.0 all-reduce.2.cloned.1.call-start
  10.8 0.8 reduce-window.9
  11.6 0.7 fusion.71
  12.3 1.4 select_reduce_fusion.2
  14.3 0.0 copy-start.5
  14.3 0.0 copy-start.6
  14.3 0.0 copy-start.8
  14.3 0.0 copy-start.9
  14.4 41.8 %all-gather.3.cloned.1.call-done = bf16[4096,512]{0,1:T(8,128)(2,1)} async-done(((bf16[512,512]{0,1:T(8,128)(2,1)}), bf16[4096,512]{0,1:T(8,128)(2,1)}) %all-gather.3.cloned.1.call-update) | async-done | bytes 4194320 | tf_op jit(solution)/shard_map/all_gather | solution.py:86
  56.2 4.2 constant_dynamic-slice_fusion.3
  60.4 3.2 collective-permute-start
  63.6 40.1 %all-gather.5.cloned.1.call-done = bf16[4096,512]{0,1:T(8,128)(2,1)} async-done(((bf16[512,512]{0,1:T(8,128)(2,1)}), bf16[4096,512]{0,1:T(8,128)(2,1)}) %all-gather.5.cloned.1.call-update) | async-done | bytes 4194320 | tf_op jit(solution)/shard_map/all_gather | solution.py:87
  103.7 4.3 constant_dynamic-slice_fusion.2
  107.9 4.5 collective-permute-start.1
  112.4 0.0 collective-permute-done
  112.4 43.7 %collective-permute-done.1 = bf16[2048,512]{0,1:T(8,128)(2,1)} collective-permute-done((bf16[2048,512]{0,1:T(8,128)(2,1)}, bf16[2048,512]{0,1:T(8,128)(2,1)}, u32[]{:S(2)}, u32[]{:S(2)}) %collective-permute-start.1) | collective-permute-done | bytes 2097184 | tf_op jit(solution)/shard_map/ppermute | solution.py:17
  156.1 0.0 copy-done.5
  156.1 0.0 copy-done.6
  156.1 0.0 copy-done.8
  156.1 0.0 copy-done.9
  156.1 251.9 %conditional.1 = (bf16[512,4096]{1,0:T(8,128)(2,1)}) conditional(s32[]{:T(128)} %convert_element_type.49, (bf16[512,4096]{1,0:T(8,128)(2,1)}, bf16[2048,512]{0,1:T(8,128)(2,1)S(1)}, bf16[128,16,512]{2,1,0:T(8,128)(2,1)}, bf16[512,512]{1,0:T(8,128)(2,1)S(1)}, s32[]{:T(128)}, /*index=5*/s32[]{:T(128)}, s32[4]{0:T(128)S(1)}, ...), branch_computations={%region_4.13_spmd.clone, %region_13.19_spmd} | conditional | flops 2720017408 | bytes 193102208 | solution.py:134
  164.7 6.7 %constant_dynamic-slice_fusion = (bf16[2560,512]{0,1:T(8,128)(2,1)S(1)}, bf16[2560,512]{0,1:T(8,128)(2,1)}) fusion(bf16[4096,512]{0,1:T(8,128)(2,1)} %get-tuple-element.223, s32[]{:T(128)S(6)} %min.8, bf16[4096,512]{0,1:T(8,128)(2,1)} %get-tuple-element.222), kind=kLoop, calls=%fused_computation.30 | loop fusion | bytes 10485764 | tf_op jit(solution)/shard_map/dynamic_slice | solution.py:94
  171.4 4.4 copy.67
  175.8 2.5 copy.68
  178.4 0.1 select_reduce_fusion
  178.4 6.5 %copy.90 = bf16[512,4096]{0,1:T(8,128)(2,1)} copy(bf16[512,4096]{1,0:T(8,128)(2,1)} %get-tuple-element.458) | data formatting | bytes 8388608 | tf_op jit(solution)/shard_map
  184.9 211.7 %while.44 = (s32[]{:T(128)}, bf16[8,512,4,128]{3,1,2,0:T(8,128)(2,1)}, bf16[8,512,4,128]{1,3,0,2:T(8,128)(2,1)}, bf16[2560,4,128]{2,0,1:T(8,128)(2,1)}, bf16[256...) while((s32[]{:T(128)}, ...), condition=%wide.region_18.18_spmd.clone, body=%wide.region_15.17_spmd.clone.sunk | while | flops 2720008704 | bytes 50887772 | solution.py:42
  184.9 1.1 compare_and_fusion.2
  186.1 13.9 %fusion.112 = (f32[4,512]{1,0:T(4,128)S(1)}, f32[4,512,2560]{2,1,0:T(8,128)}) fusion(pred[512,2560]{1,0:T(8,128)(4,1)S(1)} %compare_and_fusion.2, bf16[2560,4,128]{2,0,1:T(8,128)(2,1)} %get-tuple-element.691, bf16[8,512,4,128]{1,3,0,2:T(8,128)(2,1)} %get-tuple-element.690, s32[]{:T(128)} %get-tuple-element.679), kind=kOutput, calls=%fused_computation.94.clone.1 | convolution fusion | flops 1363151360 | bytes 25436672 | tf_op jit(solution)/shard_map/cond/branch_1_fun/while/body/eval_jaxpr/sub | solution.py:36
  200.0 11.4 %fusion.113 = bf16[8,512,4,128]{3,1,2,0:T(8,128)(2,1)} fusion(bf16[8,512,4,128]{3,1,2,0:T(8,128)(2,1)} %get-tuple-element.680, s32[]{:T(128)} %get-tuple-element.679, bf16[2560,4,128]{2,0,1:T(8,128)(2,1)} %get-tuple-element.692, f32[4,512,2560]{2,1,0:T(8,128)} %get-tuple-element.651, f32[4,512]{1,0:T(4,128)S(1)} %get-tuple-element.652), kind=kOutput, calls=%fused_computation.16.clone.1 | convolution fusion | flops 1352925184 | bytes 24125952 | tf_op jit(solution)/shard_map/cond/branch_1_fun/while/body/eval_jaxpr/krw,wkd->rkd/dot_general | solution.py:38
  211.4 1.1 compare_and_fusion.2
  212.5 13.9 %fusion.112 = (f32[4,512]{1,0:T(4,128)S(1)}, f32[4,512,2560]{2,1,0:T(8,128)}) fusion(pred[512,2560]{1,0:T(8,128)(4,1)S(1)} %compare_and_fusion.2, bf16[2560,4,128]{2,0,1:T(8,128)(2,1)} %get-tuple-element.691, bf16[8,512,4,128]{1,3,0,2:T(8,128)(2,1)} %get-tuple-element.690, s32[]{:T(128)} %get-tuple-element.679), kind=kOutput, calls=%fused_computation.94.clone.1 | convolution fusion | flops 1363151360 | bytes 25436672 | tf_op jit(solution)/shard_map/cond/branch_1_fun/while/body/eval_jaxpr/sub | solution.py:36
  226.4 11.4 %fusion.113 = bf16[8,512,4,128]{3,1,2,0:T(8,128)(2,1)} fusion(bf16[8,512,4,128]{3,1,2,0:T(8,128)(2,1)} %get-tuple-element.680, s32[]{:T(128)} %get-tuple-element.679, bf16[2560,4,128]{2,0,1:T(8,128)(2,1)} %get-tuple-element.692, f32[4,512,2560]{2,1,0:T(8,128)} %get-tuple-element.651, f32[4,512]{1,0:T(4,128)S(1)} %get-tuple-element.652), kind=kOutput, calls=%fused_computation.16.clone.1 | convolution fusion | flops 1352925184 | bytes 24125952 | tf_op jit(solution)/shard_map/cond/branch_1_fun/while/body/eval_jaxpr/krw,wkd->rkd/dot_general | solution.py:38
  237.9 1.1 compare_and_fusion.2
  239.0 13.9 %fusion.112 = (f32[4,512]{1,0:T(4,128)S(1)}, f32[4,512,2560]{2,1,0:T(8,128)}) fusion(pred[512,2560]{1,0:T(8,128)(4,1)S(1)} %compare_and_fusion.2, bf16[2560,4,128]{2,0,1:T(8,128)(2,1)} %get-tuple-element.691, bf16[8,512,4,128]{1,3,0,2:T(8,128)(2,1)} %get-tuple-element.690, s32[]{:T(128)} %get-tuple-element.679), kind=kOutput, calls=%fused_computation.94.clone.1 | convolution fusion | flops 1363151360 | bytes 25436672 | tf_op jit(solution)/shard_map/cond/branch_1_fun/while/body/eval_jaxpr/sub | solution.py:36
  252.9 11.4 %fusion.113 = bf16[8,512,4,128]{3,1,2,0:T(8,128)(2,1)} fusion(bf16[8,512,4,128]{3,1,2,0:T(8,128)(2,1)} %get-tuple-element.680, s32[]{:T(128)} %get-tuple-element.679, bf16[2560,4,128]{2,0,1:T(8,128)(2,1)} %get-tuple-element.692, f32[4,512,2560]{2,1,0:T(8,128)} %get-tuple-element.651, f32[4,512]{1,0:T(4,128)S(1)} %get-tuple-element.652), kind=kOutput, calls=%fused_computation.16.clone.1 | convolution fusion | flops 1352925184 | bytes 24125952 | tf_op jit(solution)/shard_map/cond/branch_1_fun/while/body/eval_jaxpr/krw,wkd->rkd/dot_general | solution.py:38
  264.3 1.1 compare_and_fusion.2
  265.5 13.9 %fusion.112 = (f32[4,512]{1,0:T(4,128)S(1)}, f32[4,512,2560]{2,1,0:T(8,128)}) fusion(pred[512,2560]{1,0:T(8,128)(4,1)S(1)} %compare_and_fusion.2, bf16[2560,4,128]{2,0,1:T(8,128)(2,1)} %get-tuple-element.691, bf16[8,512,4,128]{1,3,0,2:T(8,128)(2,1)} %get-tuple-element.690, s32[]{:T(128)} %get-tuple-element.679), kind=kOutput, calls=%fused_computation.94.clone.1 | convolution fusion | flops 1363151360 | bytes 25436672 | tf_op jit(solution)/shard_map/cond/branch_1_fun/while/body/eval_jaxpr/sub | solution.py:36
  279.4 11.4 %fusion.113 = bf16[8,512,4,128]{3,1,2,0:T(8,128)(2,1)} fusion(bf16[8,512,4,128]{3,1,2,0:T(8,128)(2,1)} %get-tuple-element.680, s32[]{:T(128)} %get-tuple-element.679, bf16[2560,4,128]{2,0,1:T(8,128)(2,1)} %get-tuple-element.692, f32[4,512,2560]{2,1,0:T(8,128)} %get-tuple-element.651, f32[4,512]{1,0:T(4,128)S(1)} %get-tuple-element.652), kind=kOutput, calls=%fused_computation.16.clone.1 | convolution fusion | flops 1352925184 | bytes 24125952 | tf_op jit(solution)/shard_map/cond/branch_1_fun/while/body/eval_jaxpr/krw,wkd->rkd/dot_general | solution.py:38
  290.8 1.1 compare_and_fusion.2
  291.9 13.9 %fusion.112 = (f32[4,512]{1,0:T(4,128)S(1)}, f32[4,512,2560]{2,1,0:T(8,128)}) fusion(pred[512,2560]{1,0:T(8,128)(4,1)S(1)} %compare_and_fusion.2, bf16[2560,4,128]{2,0,1:T(8,128)(2,1)} %get-tuple-element.691, bf16[8,512,4,128]{1,3,0,2:T(8,128)(2,1)} %get-tuple-element.690, s32[]{:T(128)} %get-tuple-element.679), kind=kOutput, calls=%fused_computation.94.clone.1 | convolution fusion | flops 1363151360 | bytes 25436672 | tf_op jit(solution)/shard_map/cond/branch_1_fun/while/body/eval_jaxpr/sub | solution.py:36
  305.8 11.4 %fusion.113 = bf16[8,512,4,128]{3,1,2,0:T(8,128)(2,1)} fusion(bf16[8,512,4,128]{3,1,2,0:T(8,128)(2,1)} %get-tuple-element.680, s32[]{:T(128)} %get-tuple-element.679, bf16[2560,4,128]{2,0,1:T(8,128)(2,1)} %get-tuple-element.692, f32[4,512,2560]{2,1,0:T(8,128)} %get-tuple-element.651, f32[4,512]{1,0:T(4,128)S(1)} %get-tuple-element.652), kind=kOutput, calls=%fused_computation.16.clone.1 | convolution fusion | flops 1352925184 | bytes 24125952 | tf_op jit(solution)/shard_map/cond/branch_1_fun/while/body/eval_jaxpr/krw,wkd->rkd/dot_general | solution.py:38
  317.3 1.1 compare_and_fusion.2
  318.4 13.9 %fusion.112 = (f32[4,512]{1,0:T(4,128)S(1)}, f32[4,512,2560]{2,1,0:T(8,128)}) fusion(pred[512,2560]{1,0:T(8,128)(4,1)S(1)} %compare_and_fusion.2, bf16[2560,4,128]{2,0,1:T(8,128)(2,1)} %get-tuple-element.691, bf16[8,512,4,128]{1,3,0,2:T(8,128)(2,1)} %get-tuple-element.690, s32[]{:T(128)} %get-tuple-element.679), kind=kOutput, calls=%fused_computation.94.clone.1 | convolution fusion | flops 1363151360 | bytes 25436672 | tf_op jit(solution)/shard_map/cond/branch_1_fun/while/body/eval_jaxpr/sub | solution.py:36
  332.3 11.4 %fusion.113 = bf16[8,512,4,128]{3,1,2,0:T(8,128)(2,1)} fusion(bf16[8,512,4,128]{3,1,2,0:T(8,128)(2,1)} %get-tuple-element.680, s32[]{:T(128)} %get-tuple-element.679, bf16[2560,4,128]{2,0,1:T(8,128)(2,1)} %get-tuple-element.692, f32[4,512,2560]{2,1,0:T(8,128)} %get-tuple-element.651, f32[4,512]{1,0:T(4,128)S(1)} %get-tuple-element.652), kind=kOutput, calls=%fused_computation.16.clone.1 | convolution fusion | flops 1352925184 | bytes 24125952 | tf_op jit(solution)/shard_map/cond/branch_1_fun/while/body/eval_jaxpr/krw,wkd->rkd/dot_general | solution.py:38
  343.7 1.1 compare_and_fusion.2
  344.9 13.9 %fusion.112 = (f32[4,512]{1,0:T(4,128)S(1)}, f32[4,512,2560]{2,1,0:T(8,128)}) fusion(pred[512,2560]{1,0:T(8,128)(4,1)S(1)} %compare_and_fusion.2, bf16[2560,4,128]{2,0,1:T(8,128)(2,1)} %get-tuple-element.691, bf16[8,512,4,128]{1,3,0,2:T(8,128)(2,1)} %get-tuple-element.690, s32[]{:T(128)} %get-tuple-element.679), kind=kOutput, calls=%fused_computation.94.clone.1 | convolution fusion | flops 1363151360 | bytes 25436672 | tf_op jit(solution)/shard_map/cond/branch_1_fun/while/body/eval_jaxpr/sub | solution.py:36
  358.8 11.4 %fusion.113 = bf16[8,512,4,128]{3,1,2,0:T(8,128)(2,1)} fusion(bf16[8,512,4,128]{3,1,2,0:T(8,128)(2,1)} %get-tuple-element.680, s32[]{:T(128)} %get-tuple-element.679, bf16[2560,4,128]{2,0,1:T(8,128)(2,1)} %get-tuple-element.692, f32[4,512,2560]{2,1,0:T(8,128)} %get-tuple-element.651, f32[4,512]{1,0:T(4,128)S(1)} %get-tuple-element.652), kind=kOutput, calls=%fused_computation.16.clone.1 | convolution fusion | flops 1352925184 | bytes 24125952 | tf_op jit(solution)/shard_map/cond/branch_1_fun/while/body/eval_jaxpr/krw,wkd->rkd/dot_general | solution.py:38
  370.2 1.1 compare_and_fusion.2
  371.3 13.9 %fusion.112 = (f32[4,512]{1,0:T(4,128)S(1)}, f32[4,512,2560]{2,1,0:T(8,128)}) fusion(pred[512,2560]{1,0:T(8,128)(4,1)S(1)} %compare_and_fusion.2, bf16[2560,4,128]{2,0,1:T(8,128)(2,1)} %get-tuple-element.691, bf16[8,512,4,128]{1,3,0,2:T(8,128)(2,1)} %get-tuple-element.690, s32[]{:T(128)} %get-tuple-element.679), kind=kOutput, calls=%fused_computation.94.clone.1 | convolution fusion | flops 1363151360 | bytes 25436672 | tf_op jit(solution)/shard_map/cond/branch_1_fun/while/body/eval_jaxpr/sub | solution.py:36
  385.2 11.4 %fusion.113 = bf16[8,512,4,128]{3,1,2,0:T(8,128)(2,1)} fusion(bf16[8,512,4,128]{3,1,2,0:T(8,128)(2,1)} %get-tuple-element.680, s32[]{:T(128)} %get-tuple-element.679, bf16[2560,4,128]{2,0,1:T(8,128)(2,1)} %get-tuple-element.692, f32[4,512,2560]{2,1,0:T(8,128)} %get-tuple-element.651, f32[4,512]{1,0:T(4,128)S(1)} %get-tuple-element.652), kind=kOutput, calls=%fused_computation.16.clone.1 | convolution fusion | flops 1352925184 | bytes 24125952 | tf_op jit(solution)/shard_map/cond/branch_1_fun/while/body/eval_jaxpr/krw,wkd->rkd/dot_general | solution.py:38
  396.7 4.9 copy.69
  401.6 6.2 %copy.99 = bf16[64,8,32,128]{3,1,2,0:T(8,128)(2,1)} copy(bf16[64,8,32,128]{3,2,1,0:T(8,128)(2,1)S(1)} %bitcast.147) | data formatting | bytes 8388608 | tf_op jit(solution)/shard_map/cond
  408.0 28.6 %convolution_convert_fusion.1 = bf16[512,5120]{1,0:T(8,128)(2,1)} fusion(bf16[512,4096]{1,0:T(8,128)(2,1)} %get-tuple-element.748, bf16[4096,5120]{1,0:T(8,128)(2,1)} %param.25), kind=kOutput, calls=%fused_computation.86 | convolution fusion | flops 21477457920 | bytes 51380224 | tf_op jit(solution)/shard_map/dot_general | solution.py:137
  436.6 0.0 all-reduce.2.cloned.1.call-update
  436.6 129.5 %all-reduce.2.cloned.1.call-done = bf16[512,5120]{1,0:T(8,128)(2,1)} async-done(((bf16[512,5120]{1,0:T(8,128)(2,1)}), bf16[512,5120]{1,0:T(8,128)(2,1)}) %all-reduce.2.cloned.1.call-update) | async-done | bytes 5242896 | tf_op jit(solution)/shard_map/psum | solution.py:136
  566.1 3.4 convert_convert_fusion
  (4 shorter events, 0.0 us)
Async XLA Ops:
  6.5 49.6 %all-gather.3.cloned.1.call-start = ((), (), s32[]{:S(2)}) async-start(), calls=%async_computation | async-start | bytes 4718592 | tf_op jit(solution)/shard_map/all_gather | solution.py:86
  8.6 95.1 %all-gather.5.cloned.1.call-start = ((), (), s32[]{:S(2)}) async-start(), calls=%async_computation.1 | async-start | bytes 4718592 | tf_op jit(solution)/shard_map/all_gather | solution.py:87
  10.7 555.4 %all-reduce.2.cloned.1.call-start = ((), (), s32[]{:S(2)}) async-start(), calls=%async_computation.2 | async-start | bytes 10485760 | tf_op jit(solution)/shard_map/psum | solution.py:136
  14.3 141.8 %copy-start.5 = (bf16[512,512]{1,0:T(8,128)(2,1)S(1)}, bf16[512,512]{1,0:T(8,128)(2,1)}, u32[]{:S(2)}) copy-start(bf16[512,512]{1,0:T(8,128)(2,1)} %param.18) | copy-start | bytes 1572868
  14.3 141.8 %copy-start.6 = (bf16[512,512]{1,0:T(8,128)(2,1)S(1)}, bf16[512,512]{1,0:T(8,128)(2,1)}, u32[]{:S(2)}) copy-start(bf16[512,512]{1,0:T(8,128)(2,1)} %param.19) | copy-start | bytes 1572868
  14.3 141.8 %copy-start.8 = (s32[4]{0:T(128)S(1)}, s32[4]{0:T(128)}, u32[]{:S(2)}) copy-start(s32[4]{0:T(128)} %param.23) | copy-start | bytes 52
  14.3 141.8 %copy-start.9 = (s32[128]{0:T(128)S(1)}, s32[128]{0:T(128)}, u32[]{:S(2)}) copy-start(s32[128]{0:T(128)} %param.22) | copy-start | bytes 1540
  60.4 52.0 %collective-permute-start = (bf16[2048,512]{0,1:T(8,128)(2,1)}, bf16[2048,512]{0,1:T(8,128)(2,1)S(1)}, u32[]{:S(2)}, u32[]{:S(2)}) collective-permute-start(bf16[2048,512]{0,1:T(8,128)(2,1)} %constant_dynamic-slice_fusion.3), channel_id=1, source_target_pairs={{0,16},{1,17},{2,18},{3,19},{4,20},{5,21},{6,22},{7,23},{8,24},{9,... | collective-permute-start | bytes 6291464 | tf_op jit(solution)/shard_map/ppermute | solution.py:17
  107.9 48.2 %collective-permute-start.1 = (bf16[2048,512]{0,1:T(8,128)(2,1)}, bf16[2048,512]{0,1:T(8,128)(2,1)}, u32[]{:S(2)}, u32[]{:S(2)}) collective-permute-start(bf16[2048,512]{0,1:T(8,128)(2,1)} %constant_dynamic-slice_fusion.2), channel_id=1, source_target_pairs={{0,16},{1,17},{2,18},{3,19},{4,20},{5,21},{6,22},{7,23},{8,24},{9,... | collective-permute-start | bytes 6291464 | tf_op jit(solution)/shard_map/ppermute | solution.py:17
Sparse Core Ops, SparseCore 0:
  9.0 47.1 all-gather.2
  57.8 45.8 all-gather.4
  436.8 129.3 all-reduce.1
where the time goes:
time: 584 us; the launch traced here: 576 us
  waiting for transfers between devices  255 us (44%)
  matrix products  231 us (40%)
  local copies, waits for them, and re-layouts  43.8 us (8%)
  other arithmetic  15.4 us (3%)
  between operations  14.1 us (2%)
  loops' own time  8.91 us (2%)
  starting transfers between devices  7.77 us (1%)
    psum x1, waiting for transfers between devices, on_device(): lax.psum(jnp.dot(mixed, out_weight, preferred_element_type=jnp.float32).a...  129 us
    sub x8, matrix products, one_group(): exponent = jnp.exp(scores - row_max)  111 us
    dot_general x8, matrix products, one_group(): jnp.einsum('krw,wkd->rkd', weights, value_heads, preferred_element_type=j...  91.4 us
    ppermute x2, waiting for transfers between devices, shifted(): return lax.ppermute(array, axis, pairs)  43.7 us
    all_gather x1, waiting for transfers between devices, on_device(): lax.all_gather(key_rows, 'dp', axis=0, tiled=True)  41.8 us
    all_gather x1, waiting for transfers between devices, on_device(): lax.all_gather(rows_of_values, 'dp', axis=0, tiled=True)  40.1 us
    dot_general x1, matrix products, on_device(): jnp.dot(mixed, out_weight, preferred_element_type=jnp.float32)  28.6 us
    cond x3, local copies, waits for them, and re-layouts  13.1 us
  transfers between devices with their start and end apart: 5, of which 4 were waited for; matrix products, arithmetic and copies ran while one was open for 2% of the time, Pallas kernels for 0%

commit v1 on v0

v1 whole, which is shorter than its diff:
```python
import functools

import jax
import jax.numpy as jnp
from jax import lax
from jax.experimental import pallas as pl
from jax.experimental.pallas import tpu as pltpu
from jax.sharding import PartitionSpec as P

HEAD_SIZE = 128
STEPS = 4
MAXLEN = 2048
GROUP = 8
WIDE = GROUP * HEAD_SIZE
ROWS = 128
KEYS = 512
SLOTS = 8

masked_score = -1e30
SCALE = HEAD_SIZE ** (-0.5)
SCALE2 = SCALE * 1.4426950408889634
VMEM = 48 * 1024 * 1024
NT = (((1,), (1,)), ((), ()))


def stacked_heads(q_ref, rows, heads):
    return jnp.concatenate(
        [q_ref[rows, g * HEAD_SIZE : (g + 1) * HEAD_SIZE] for g in heads], axis=0
    )


def prefill_kernel(bounds_ref, qpos_ref, qstart_ref, q_ref, k_ref, v_ref, o_ref, m_ref, acc_ref, vx_ref, *, row_base):
    step = pl.program_id(1)
    chunk = row_base + step
    window = k_ref.shape[0]
    parts = 2
    per = GROUP // parts

    @pl.when(step == 0)
    def _():
        vx_ref[:, :HEAD_SIZE] = v_ref[...]
        lane = lax.broadcasted_iota(jnp.int32, (window, HEAD_SIZE), 1)
        vx_ref[:, HEAD_SIZE:] = jnp.where(lane == 0, 1.0, 0.0).astype(jnp.bfloat16)

    m_ref[...] = jnp.full_like(m_ref, masked_score)
    acc_ref[...] = jnp.zeros_like(acc_ref)
    low, clear, diagonal, high = [bounds_ref[4 * chunk + i] for i in range(4)]

    def visit(c, masked):
        at = pl.multiple_of(c * KEYS, KEYS)
        keys = k_ref[pl.ds(at, KEYS), :]
        values = vx_ref[pl.ds(at, KEYS), :]
        if masked:
            pos = at + lax.broadcasted_iota(jnp.int32, (ROWS, KEYS), 1)
            allowed = (pos >= qstart_ref[...]) & (pos <= qpos_ref[...])
            bias = jnp.where(allowed, 0.0, masked_score)
            bias = jnp.concatenate([bias] * per, axis=0)
        for part in range(parts):
            q = stacked_heads(q_ref, slice(None), range(part * per, (part + 1) * per))
            s = lax.dot_general(q, keys, NT, preferred_element_type=jnp.float32)
            if masked:
                s = jnp.where(bias < 0, masked_score, s)
            m_old = m_ref[part]
            m_new = jnp.maximum(m_old, jnp.max(s, axis=1, keepdims=True))
            p = jnp.exp2((s - m_new[:, :1]) * SCALE2).astype(jnp.bfloat16)
            alpha = jnp.exp2((m_old - m_new) * SCALE2)
            acc_ref[part] = acc_ref[part] * alpha[:, :1] + lax.dot_general(
                p, values, (((1,), (0,)), ((), ())), preferred_element_type=jnp.float32
            )
            m_ref[part] = m_new

    lax.fori_loop(low, clear, lambda c, _: (visit(c, True), 0)[1], 0)
    lax.fori_loop(clear, diagonal, lambda c, _: (visit(c, False), 0)[1], 0)
    lax.fori_loop(diagonal, high, lambda c, _: (visit(c, True), 0)[1], 0)
    for g in range(GROUP):
        part, rows = g // per, slice((g % per) * ROWS, (g % per + 1) * ROWS)
        total = acc_ref[part, rows, HEAD_SIZE : HEAD_SIZE + 1]
        o_ref[:, g * HEAD_SIZE : (g + 1) * HEAD_SIZE] = (
            acc_ref[part, rows, :HEAD_SIZE] / total
        ).astype(o_ref.dtype)


def prefill_attend(bounds, qpos, qstart, queries, window, first_head, heads, row_base, row_count):
    chunks = row_count // ROWS
    length = window.shape[0]
    parts = 2
    return pl.pallas_call(
        functools.partial(prefill_kernel, row_base=row_base),
        grid_spec=pltpu.PrefetchScalarGridSpec(
            num_scalar_prefetch=1,
            grid=(heads, chunks),
            in_specs=[
                pl.BlockSpec((ROWS, 1), lambda h, i, b: (row_base + i, 0)),
                pl.BlockSpec((ROWS, 1), lambda h, i, b: (row_base + i, 0)),
                pl.BlockSpec((ROWS, WIDE), lambda h, i, b: (row_base + i, first_head + h)),
                pl.BlockSpec((length, HEAD_SIZE), lambda h, i, b: (0, h)),
                pl.BlockSpec((length, HEAD_SIZE), lambda h, i, b: (0, heads + h)),
            ],
            out_specs=pl.BlockSpec((ROWS, WIDE), lambda h, i, b: (i, h)),
            scratch_shapes=[
                pltpu.VMEM((parts, ROWS * GROUP // parts, HEAD_SIZE), jnp.float32),
                pltpu.VMEM((parts, ROWS * GROUP // parts, 2 * HEAD_SIZE), jnp.float32),
                pltpu.VMEM((length, 2 * HEAD_SIZE), jnp.bfloat16),
            ],
        ),
        out_shape=jax.ShapeDtypeStruct((row_count, heads * WIDE), jnp.bfloat16),
        compiler_params=pltpu.CompilerParams(vmem_limit_bytes=VMEM),
        cost_estimate=pl.CostEstimate(
            flops=heads * GROUP * row_count * 2048 * 512,
            bytes_accessed=heads * row_count * WIDE * 4,
            transcendentals=heads * GROUP * row_count * 2048,
        ),
        name="prefill_attend",
    )(bounds, qpos, qstart, queries, window, window)


def decode_kernel(valid_ref, q_ref, k_ref, v_ref, ck_ref, cv_ref, o_ref):
    positions = ck_ref.shape[1]
    rows = SLOTS * STEPS
    held = SLOTS * positions
    stack = rows * GROUP

    def grid_of(shape, axis):
        return lax.broadcasted_iota(jnp.int32, shape, axis)

    row_a = grid_of((stack, held), 0) % rows
    same = row_a // STEPS == grid_of((stack, held), 1) // positions
    row_b = grid_of((stack, rows), 0) % rows
    col_b = grid_of((stack, rows), 1)
    own = (row_b // STEPS == col_b // STEPS) & (col_b <= row_b)
    for part in range(ROWS // rows):
        span = slice(part * rows, (part + 1) * rows)
        slots = slice(part * SLOTS, (part + 1) * SLOTS)
        q = stacked_heads(q_ref, span, range(GROUP))
        cached = ck_ref[slots].reshape(held, HEAD_SIZE)
        cached_values = cv_ref[slots].reshape(held, HEAD_SIZE)
        s_a = lax.dot_general(q, cached, NT, preferred_element_type=jnp.float32)
        s_b = lax.dot_general(q, k_ref[span, :], NT, preferred_element_type=jnp.float32)
        s_a = jnp.where(same & (valid_ref[0, part : part + 1, :] > 0), s_a, masked_score)
        s_b = jnp.where(own, s_b, masked_score)
        top = jnp.maximum(jnp.max(s_a, axis=1, keepdims=True), jnp.max(s_b, axis=1, keepdims=True))
        p_a = jnp.exp2((s_a - top) * SCALE2)
        p_b = jnp.exp2((s_b - top) * SCALE2)
        total = jnp.sum(p_a, axis=1, keepdims=True) + jnp.sum(p_b, axis=1, keepdims=True)
        out = jnp.dot(p_a.astype(jnp.bfloat16), cached_values, preferred_element_type=jnp.float32)
        out += jnp.dot(p_b.astype(jnp.bfloat16), v_ref[span, :], preferred_element_type=jnp.float32)
        out = (out / total).astype(o_ref.dtype)
        for g in range(GROUP):
            o_ref[span, g * HEAD_SIZE : (g + 1) * HEAD_SIZE] = out[g * rows : (g + 1) * rows]


def decode_attend(valid, queries, keys, values, cached_keys, cached_values, first_head, heads, row_base, row_count):
    positions = cached_keys.shape[1]
    slots = ROWS // STEPS
    parts = ROWS // (SLOTS * STEPS)
    return pl.pallas_call(
        decode_kernel,
        grid=(heads, row_count // ROWS),
        in_specs=[
            pl.BlockSpec((1, parts, SLOTS * positions), lambda h, i: (row_base + i, 0, 0)),
            pl.BlockSpec((ROWS, WIDE), lambda h, i: (row_base + i, first_head + h)),
            pl.BlockSpec((ROWS, HEAD_SIZE), lambda h, i: (row_base + i, first_head + h)),
            pl.BlockSpec((ROWS, HEAD_SIZE), lambda h, i: (row_base + i, first_head + h)),
            pl.BlockSpec((slots, positions, HEAD_SIZE), lambda h, i: (row_base + i, 0, first_head + h)),
            pl.BlockSpec((slots, positions, HEAD_SIZE), lambda h, i: (row_base + i, 0, first_head + h)),
        ],
        out_specs=pl.BlockSpec((ROWS, WIDE), lambda h, i: (i, h)),
        out_shape=jax.ShapeDtypeStruct((row_count, heads * WIDE), jnp.bfloat16),
        compiler_params=pltpu.CompilerParams(vmem_limit_bytes=VMEM),
        cost_estimate=pl.CostEstimate(
            flops=heads * GROUP * row_count * 2048 * 512,
            bytes_accessed=heads * row_count * WIDE * 4,
            transcendentals=heads * GROUP * row_count * 2048,
        ),
        name="decode_attend",
    )(valid, queries, keys, values, cached_keys, cached_values)


def project_kernel(base_ref, *refs):
    parts, w_ref, o_ref = refs[:-2], refs[-2], refs[-1]
    total, depth = None, 0
    for part in parts:
        count = part.shape[1]
        product = jnp.dot(
            part[...], w_ref[depth : depth + count, :], preferred_element_type=jnp.float32
        )
        total = product if total is None else total + product
        depth += count
    o_ref[...] = total.astype(o_ref.dtype)


def project(parts, row_blocks, row_count, weight, base, columns):
    tile = [c for c in (512, 640, 256, 128) if columns % c == 0][0]
    tiles = columns // tile
    depth = weight.shape[0]
    specs = [
        pl.BlockSpec((row_count, part.shape[1]), lambda j, b, block=block: (block, 0))
        for part, block in zip(parts, row_blocks)
    ]
    return pl.pallas_call(
        project_kernel,
        grid_spec=pltpu.PrefetchScalarGridSpec(
            num_scalar_prefetch=1,
            grid=(tiles,),
            in_specs=specs + [pl.BlockSpec((depth, tile), lambda j, b: (0, b[0] * tiles + j))],
            out_specs=pl.BlockSpec((row_count, tile), lambda j, b: (0, j)),
        ),
        out_shape=jax.ShapeDtypeStruct((row_count, columns), jnp.bfloat16),
        compiler_params=pltpu.CompilerParams(vmem_limit_bytes=VMEM),
        cost_estimate=pl.CostEstimate(
            flops=2 * row_count * depth * columns,
            bytes_accessed=2 * depth * columns,
            transcendentals=0,
        ),
        name="project",
    )(base, *parts, weight)


def on_device(
    query_rows,
    key_rows,
    rows_of_values,
    cached_key_rows,
    cached_value_rows,
    cache_lengths,
    prompt_lengths,
    owners,
    out_weight,
):
    row_count = query_rows.shape[0]
    count = lax.axis_size("dp")
    heads = key_rows.shape[1] // HEAD_SIZE
    position = lax.axis_index("dp")
    section = lax.axis_index("section")
    first_section = section == 0
    core = position % 2
    chip = position // 2
    first_row = position * row_count
    starts = jnp.cumsum(prompt_lengths) - prompt_lengths
    ends = starts + prompt_lengths

    def up(array, by):
        return lax.ppermute(array, ("section", "dp"), [(i, i + by) for i in range(count - by)])

    def partner(array):
        return lax.ppermute(array, ("section", "dp"), [(i, i ^ 1) for i in range(count)])

    def across(array):
        return lax.ppermute(array, ("section", "dp"), [(i, i + count) for i in range(count)])

    split = [heads // 2, heads - heads // 2] if heads > 1 else [heads]
    packed, first = [], 0
    for width in split:
        cols = slice(first * HEAD_SIZE, (first + width) * HEAD_SIZE)
        packed.append(jnp.concatenate([key_rows[:, cols], rows_of_values[:, cols]], 1))
        first += width

    reach = MAXLEN // row_count
    hops = -(-reach // 2)

    def window_of(block):
        far = [up(block, 2 * hop) for hop in range(hops, 0, -1)] + [block]
        pieces = []
        for piece in far:
            other = partner(piece)
            pieces += [jnp.where(core == 0, piece, other), jnp.where(core == 0, other, piece)]
        return jnp.concatenate(pieces, 0)

    windows = [window_of(block) for block in packed]
    window_start = (chip - hops) * 2 * row_count

    prompt_block = [across(block) for block in packed]
    gathered = lax.all_gather(query_rows[:STEPS], "dp", axis=0, tiled=False)
    row = first_row + jnp.arange(row_count, dtype=jnp.int32)
    inside = (row[None] >= starts[:, None]) & (row[None] < ends[:, None])
    owner_of_row = jnp.sum(jnp.where(inside, owners[:, None], 0), axis=0)

    def fresh_part():
        keys = jnp.concatenate([b[:, : b.shape[1] // 2] for b in prompt_block], 1)
        values = jnp.concatenate([b[:, b.shape[1] // 2 :] for b in prompt_block], 1)
        keys = keys.reshape(row_count, heads, HEAD_SIZE)
        values = values.reshape(row_count, heads, HEAD_SIZE)
        q = gathered.reshape(count, STEPS, heads, GROUP, HEAD_SIZE)
        s = jnp.einsum("oskgd,wkd->kosgw", q, keys, preferred_element_type=jnp.float32) * SCALE
        ok = owner_of_row[None] == jnp.arange(count, dtype=jnp.int32)[:, None]
        ok = ok[None, :, None, None, :]
        s = jnp.where(ok, s, masked_score)
        top = jnp.max(s, axis=-1)
        p = jnp.where(ok, jnp.exp(s - top[..., None]), 0.0)
        total = jnp.sum(p, axis=-1)
        out = jnp.einsum(
            "kosgw,wkd->oskgd", p.astype(jnp.bfloat16), values, preferred_element_type=jnp.float32
        )
        top = jnp.transpose(top, (1, 2, 0, 3)).reshape(count, STEPS, -1)
        total = jnp.transpose(total, (1, 2, 0, 3)).reshape(count, STEPS, -1)
        return jnp.concatenate([out.reshape(count, STEPS, -1), top, total], -1)

    q_heads = heads * GROUP
    packet = q_heads * (HEAD_SIZE + 2)
    partials = lax.cond(
        first_section, lambda: jnp.zeros((count, STEPS, packet), jnp.float32), fresh_part
    )
    mine = [lax.dynamic_index_in_dim(partials, position, 0, keepdims=False)]
    for by in range(1, count):
        sent = lax.dynamic_index_in_dim(partials, (position + by) % count, 0, keepdims=False)
        mine.append(
            lax.ppermute(
                sent,
                ("section", "dp"),
                [(count + i, count + (i + by) % count) for i in range(count)],
            )
        )

    def fresh_rows():
        parts = jnp.stack(mine)
        outs = parts[..., : q_heads * HEAD_SIZE].reshape(count, STEPS, q_heads, HEAD_SIZE)
        tops = parts[..., q_heads * HEAD_SIZE : q_heads * (HEAD_SIZE + 1)]
        totals = parts[..., q_heads * (HEAD_SIZE + 1) :]
        has_new = jnp.sum((owners == position).astype(jnp.int32)) > 0
        cache_size = cached_key_rows.shape[1]
        keys = jnp.concatenate([cached_key_rows[0], key_rows[:STEPS]], 0).reshape(-1, heads, HEAD_SIZE)
        values = jnp.concatenate([cached_value_rows[0], rows_of_values[:STEPS]], 0)
        values = values.reshape(-1, heads, HEAD_SIZE)
        q = query_rows[:STEPS].reshape(STEPS, heads, GROUP, HEAD_SIZE)
        s = jnp.einsum("skgd,wkd->skgw", q, keys, preferred_element_type=jnp.float32) * SCALE
        pos = jnp.arange(cache_size + STEPS, dtype=jnp.int32)
        limit = jnp.where(has_new, 0, cache_lengths[0])
        ok = (pos[None] < jnp.minimum(limit, cache_size)) | (
            (pos[None] >= cache_size)
            & (pos[None] - cache_size <= jnp.arange(STEPS, dtype=jnp.int32)[:, None])
        )
        s = jnp.where(ok[:, None, None, :], s, masked_score).reshape(STEPS, q_heads, -1)
        top = jnp.maximum(jnp.max(s, axis=-1), jnp.max(tops, axis=0))
        p = jnp.exp(s - top[..., None])
        gains = jnp.where(totals > 0, jnp.exp(jnp.minimum(tops - top, 0.0)), 0.0)
        total = jnp.sum(p, axis=-1) + jnp.sum(totals * gains, axis=0)
        out = jnp.einsum(
            "skgw,wkd->skgd",
            p.astype(jnp.bfloat16).reshape(STEPS, heads, GROUP, -1),
            values,
            preferred_element_type=jnp.float32,
        ).reshape(STEPS, q_heads, HEAD_SIZE)
        out = out + jnp.sum(outs * gains[..., None], axis=0)
        return (out / total[..., None]).astype(jnp.bfloat16).reshape(STEPS, -1)

    query_start = jnp.max(jnp.where(starts[None, :] <= row[:, None], starts[None, :], 0), axis=1)
    qpos = (row - window_start)[:, None]
    qstart = (query_start - window_start)[:, None]
    by_chunk = (query_start - window_start).reshape(-1, ROWS)
    chunk_first = row.reshape(-1, ROWS)[:, 0] - window_start
    high = (chunk_first + ROWS - 1) // KEYS + 1
    low = jnp.clip(jnp.min(by_chunk, axis=1) // KEYS, 0, high)
    clear = jnp.clip((jnp.max(by_chunk, axis=1) + KEYS - 1) // KEYS, low, high)
    diagonal = jnp.clip(chunk_first // KEYS, clear, high)
    bounds = jnp.stack([low, clear, diagonal, high], 1).reshape(-1).astype(jnp.int32)

    cache_size = cached_key_rows.shape[1]
    valid = jnp.arange(cache_size, dtype=jnp.int32)[None] < cache_lengths[:, None]
    valid = valid.astype(jnp.float32).reshape(row_count // ROWS, -1, SLOTS * cache_size)

    def attend(half, row_base, rows, tied=None):
        first_head = sum(split[:half])
        width = split[half]

        def prefill():
            return prefill_attend(
                bounds, qpos, qstart, query_rows, windows[half], first_head, width, row_base, rows
            )

        def decode():
            out = decode_attend(
                valid, query_rows, key_rows, rows_of_values, cached_key_rows, cached_value_rows,
                first_head, width, row_base, rows,
            )
            return out

        return lax.cond(first_section, prefill, decode)

    def with_fresh(out, half):
        first_head = sum(split[:half])
        cols = slice(first_head * WIDE, (first_head + split[half]) * WIDE)
        rows = jnp.where(first_section, out[:STEPS], fresh[:, cols])
        return lax.dynamic_update_slice(out, rows, (0, 0))

    early = [attend(0, 0, row_count)] if len(split) > 1 else []
    fresh = lax.cond(
        first_section, lambda: jnp.zeros((STEPS, q_heads * HEAD_SIZE), jnp.bfloat16), fresh_rows
    )
    early = [with_fresh(early[0], 0)] if early else []
    ranks = lax.axis_size("tensor")
    rank = lax.axis_index("tensor")
    columns = out_weight.shape[1] // ranks
    half_rows = row_count // 2
    done = []
    for block in range(2):
        late = attend(len(split) - 1, block * half_rows // ROWS, half_rows)
        if block == 0:
            late = with_fresh(late, len(split) - 1)
        parts = early + [late]
        blocks = [block] * len(early) + [0]
        arrived = []
        for by in range(1, ranks):
            to = (rank + by) % ranks
            part = project(parts, blocks, half_rows, out_weight, to.reshape(1), columns)
            arrived.append(
                lax.ppermute(part, "tensor", [(i, (i + by) % ranks) for i in range(ranks)])
            )
        own = project(parts, blocks, half_rows, out_weight, rank.reshape(1), columns)
        done.append((own, arrived))
    outs = []
    for own, arrived in done:
        total = own.astype(jnp.float32)
        for part in arrived:
            total = total + part.astype(jnp.float32)
        outs.append(total.astype(jnp.bfloat16))
    return jnp.concatenate(outs, 0)


def solution(mesh):
    placed = (
        P(("section", "dp"), "tensor"),
        P(("section", "dp"), "tensor"),
        P(("section", "dp"), "tensor"),
        P("dp", None, "tensor"),
        P("dp", None, "tensor"),
        P("dp"),
        P(),
        P(),
        P("tensor", None),
    )
    return jax.shard_map(
        on_device,
        mesh=mesh,
        in_specs=placed,
        out_specs=P(("section", "dp"), "tensor"),
        check_vma=False,
    )
```

time: 584 us -> 277 us (0.47); the launches traced: 576 us -> 276 us
  waiting for transfers between devices: 255 us -> 8.58 us
  matrix products: 231 us -> 0 us
  Pallas kernels: 0 us -> 154 us
  blocking collectives: 0 us -> 44 us
  starting transfers between devices: 7.77 us -> 37.6 us
  local copies, waits for them, and re-layouts: 43.8 us -> 15.5 us
  between operations: 14.1 us -> 0.66 us
  loops' own time: 8.91 us -> 0.17 us
    pallas_call x0 -> x7, Pallas kernels: none -> 154 us  [the longest x3 110 us: prefill_attend(): pl.pallas_call(functools.partial(prefill_kernel, row_base=row_base), grid...]
    psum x1 -> x0, waiting for transfers between devices: 129 us -> none  [on_device(): lax.psum(jnp.dot(mixed, out_weight, preferred_element_type=jnp.float32).a...]
    dot_general x9 -> x0, matrix products: 120 us -> none  [the longest x8 91.4 us: one_group(): jnp.einsum('krw,wkd->rkd', weights, value_heads, preferred_element_type=j...]
    sub x8 -> x0, matrix products: 111 us -> none  [one_group(): exponent = jnp.exp(scores - row_max)]
    all_gather x2 -> x0, waiting for transfers between devices: 81.9 us -> none  [the longest x1 41.8 us: on_device(): lax.all_gather(key_rows, 'dp', axis=0, tiled=True)]
    all_gather x0 -> x1, blocking collectives: none -> 44 us  [on_device(): gathered = lax.all_gather(query_rows[:STEPS], 'dp', axis=0, tiled=False)]
    ppermute x2 -> x21, waiting for transfers between devices: 43.7 us -> 8.58 us  [the longest x4 8.53 us: up(): lax.ppermute(array, ('section', 'dp'), [(i, i + by) for i in range(count...]
    ppermute x2 -> x21, starting transfers between devices: 7.69 us -> 37.6 us  [the longest x4 14.7 us: up(): lax.ppermute(array, ('section', 'dp'), [(i, i + by) for i in range(count...]
  transfers between devices with their start and end apart: 5 -> 21, of which waited for: 4 -> 2; matrix products, arithmetic and copies ran while one was open for 2% -> 5% of each run, Pallas kernels for 0% -> 32%
where the time goes in v1:
time: 277 us; the launch traced here: 276 us
  Pallas kernels  154 us (56%)
  blocking collectives  44 us (16%)
  starting transfers between devices  37.6 us (14%)
  local copies, waits for them, and re-layouts  15.5 us (6%)
  other arithmetic  15.5 us (6%)
  waiting for transfers between devices  8.58 us (3%)
    pallas_call x3, Pallas kernels, prefill_attend(): pl.pallas_call(functools.partial(prefill_kernel, row_base=row_base), grid...  110 us
    all_gather x1, blocking collectives, on_device(): gathered = lax.all_gather(query_rows[:STEPS], 'dp', axis=0, tiled=False)  44 us
    pallas_call x4, Pallas kernels, project(): pl.pallas_call(project_kernel, grid_spec=pltpu.PrefetchScalarGridSpec(num...  43.7 us
    ppermute x4, starting transfers between devices, up(): lax.ppermute(array, ('section', 'dp'), [(i, i + by) for i in range(count...  14.7 us
    ppermute x6, starting transfers between devices, partner(): lax.ppermute(array, ('section', 'dp'), [(i, i ^ 1) for i in range(count)])  14 us
    ppermute x4, waiting for transfers between devices, up(): lax.ppermute(array, ('section', 'dp'), [(i, i + by) for i in range(count...  8.53 us
    unnamed x10, other arithmetic  8.39 us
    cond x8, local copies, waits for them, and re-layouts  5.9 us
  transfers between devices with their start and end apart: 21, of which 2 were waited for; matrix products, arithmetic and copies ran while one was open for 5% of the time, Pallas kernels for 32%

profile of v1, /device:TPU:11, one launch (start us, length us, event | category | flops | bytes accessed | tf_op | source)
XLA Modules:
  0.0 275.9 jit_solution(9954204113694913751)
XLA Ops:
  0.0 1.3 fusion.39
  1.3 0.8 pad_maximum_fusion.3
  2.1 5.0 %collective-permute-start = (bf16[512,512]{1,0:T(8,128)(2,1)}, bf16[512,512]{1,0:T(8,128)(2,1)}, u32[]{:S(2)}, u32[]{:S(2)}) collective-permute-start(bf16[512,512]{1,0:T(8,128)(2,1)} %pad_maximum_fusion.3), channel_id=1, source_target_pairs={{0,4},{1,5},{2,6},{3,7},{8,12},{9,13},{10,14},{11,15}} | collective-permute-start | bytes 1572872 | tf_op jit(solution)/shard_map/ppermute | solution.py:243
  7.2 1.3 collective-permute-start.5
  8.5 0.8 pad_maximum_fusion.4
  9.3 1.3 collective-permute-start.6
  10.6 3.3 %collective-permute-start.14 = (bf16[512,512]{1,0:T(8,128)(2,1)}, bf16[512,512]{1,0:T(8,128)(2,1)}, u32[]{:S(2)}, u32[]{:S(2)}) collective-permute-start(bf16[512,512]{1,0:T(8,128)(2,1)} %pad_maximum_fusion.4), channel_id=1, source_target_pairs={{0,4},{1,5},{2,6},{3,7},{8,12},{9,13},{10,14},{11,15}} | collective-permute-start | bytes 1572872 | tf_op jit(solution)/shard_map/ppermute | solution.py:243
  14.3 0.2 reduce-window.8
  14.5 0.9 slice_bitcast_fusion.3
  15.4 44.0 %all-gather.1 = bf16[8,4,4096]{2,1,0:T(4,128)(2,1)S(1)} all-gather(bf16[1,4,4096]{2,1,0:T(4,128)(2,1)S(1)} %slice_bitcast_fusion.3), channel_id=2, replica_groups=mesh['section'=2,'tensor'=2,'dp'=8] {'dp'}, dimensions={0}, use_global_device_ids=true | all-gather | bytes 294912 | tf_op jit(solution)/shard_map/all_gather | solution.py:273
  59.3 0.5 bitcast_subtract_fusion
  60.0 0.3 constant_dynamic-slice_fusion
  60.3 0.7 collective-permute-start.7
  61.0 0.7 collective-permute-start.8
  61.7 0.7 collective-permute-start.9
  62.4 0.7 select_reduce_fusion.1
  63.2 4.5 %collective-permute-start.2 = (bf16[512,512]{1,0:T(8,128)(2,1)}, bf16[512,512]{1,0:T(8,128)(2,1)S(1)}, u32[]{:S(2)}, u32[]{:S(2)}) collective-permute-start(bf16[512,512]{1,0:T(8,128)(2,1)} %pad_maximum_fusion.3), channel_id=1, source_target_pairs={{0,2},{1,3},{2,4},{3,5},{4,6},{5,7},{8,10},{9,11},{10,12},{11,13},... | collective-permute-start | bytes 1572872 | tf_op jit(solution)/shard_map/ppermute | solution.py:243
  67.6 1.9 collective-permute-start.16
  69.6 0.7 collective-permute-start.10
  70.3 2.4 collective-permute-start.15
  72.6 0.1 bitcast_reduce_fusion
  72.8 0.7 collective-permute-start.11
  73.6 0.7 collective-permute-start.12
  74.4 0.7 reshape.391
  75.1 0.7 collective-permute-start.13
  75.8 2.0 collective-permute-start.4
  77.8 2.4 collective-permute-start.18
  80.3 2.8 %collective-permute-start.1 = (bf16[512,512]{1,0:T(8,128)(2,1)}, bf16[512,512]{1,0:T(8,128)(2,1)}, u32[]{:S(2)}, u32[]{:S(2)}) collective-permute-start(bf16[512,512]{1,0:T(8,128)(2,1)} %collective-permute-done), channel_id=1, source_target_pairs={{0,1},{1,0},{2,3},{3,2},{4,5},{5,4},{6,7},{7,6},{8,9},{9,8},{10,11... | collective-permute-start | bytes 1572872 | tf_op jit(solution)/shard_map/ppermute | solution.py:246
  83.1 8.4 %collective-permute-done.16 = bf16[512,512]{1,0:T(8,128)(2,1)S(1)} collective-permute-done((bf16[512,512]{1,0:T(8,128)(2,1)}, bf16[512,512]{1,0:T(8,128)(2,1)S(1)}, u32[]{:S(2)}, u32[]{:S(2)}) %collective-permute-start.16) | collective-permute-done | bytes 524320 | tf_op jit(solution)/shard_map/ppermute | solution.py:243
  91.5 2.6 collective-permute-start.3
  94.1 1.9 collective-permute-start.17
  96.0 1.3 select_dynamic-update-slice_fusion.5
  97.4 1.3 select_dynamic-update-slice_fusion.4
  99.4 2.8 %copy-done.15 = bf16[512,4096]{1,0:T(8,128)(2,1)S(1)} copy-done((bf16[512,4096]{1,0:T(8,128)(2,1)S(1)}, bf16[512,4096]{1,0:T(8,128)(2,1)}, u32[]{:S(2)}) %copy-start.15) | copy-done | bytes 4194328
  102.2 0.1 copy-done.2
  102.4 31.0 %conditional.9 = (bf16[256,2048]{1,0:T(8,128)(2,1)S(1)}) conditional(s32[]{:T(128)} %convert_element_type.53, (f32[4,4,128]{2,1,0:T(4,128)S(1)}, bf16[512,4096]{1,0:T(8,128)(2,1)S(1)}, bf16[512,512]{1,0:T(8,128)(2,1)S(1)}, bf16[512,512]{1,0:T(8,128)(2,1)S(1)}, bf16[128,16,512]{2,1,0:T(8,128)(2,1)S(1)}, ...), branch_computations={%region_21.22_spmd, %region_22.23_spmd} | conditional | flops 4294967296 | bytes 31461440 | solution.py:377
  102.4 1.7 copy-done.6
  104.2 1.2 copy-done.17
  105.5 27.9 %prefill_attend.5 = bf16[256,2048]{1,0:T(8,128)(2,1)S(1)} custom-call(s32[16]{0:T(128)S(1)} %get-tuple-element.329.bounds_ref, s32[512,1]{1,0:T(8,128)S(1)} %get-tuple-element.330.qpos_ref, s32[512,1]{1,0:T(8,128)S(1)} %copy.89.qstart_ref, bf16[512,4096]{1,0:T(8,128)(2,1)} %copy-done.17, bf16[3072,512]{1,0:T(8,128)(2,1)} %copy-done.6, ...), custom_call_target="tpu_custom_call" | custom-call | flops 4294967296 | bytes 2097152 | tf_op jit(solution)/shard_map/cond/branch_1_fun/prefill_attend/pallas_call | solution.py:87
  133.4 29.4 %conditional.8 = (bf16[256,2048]{1,0:T(8,128)(2,1)}, bf16[4,2048]{1,0:T(4,128)(2,1)S(1)}) conditional(s32[]{:T(128)} %convert_element_type.53, (f32[4,4,128]{2,1,0:T(4,128)S(1)}, bf16[512,4096]{1,0:T(8,128)(2,1)}, bf16[512,512]{1,0:T(8,128)(2,1)S(1)}, bf16[512,512]{1,0:T(8,128)(2,1)}, bf16[128,16,512]{2,1,0:T(8,128)(2,1)}, ...), branch_computations={%region_19.20_spmd, %region_20.21_spmd} | conditional | flops 4294967296 | bytes 2134032 | solution.py:377
  133.6 28.5 %prefill_attend.4 = bf16[256,2048]{1,0:T(8,128)(2,1)} custom-call(s32[16]{0:T(128)S(1)} %get-tuple-element.318.bounds_ref, s32[512,1]{1,0:T(8,128)S(1)} %get-tuple-element.319.qpos_ref, s32[512,1]{1,0:T(8,128)S(1)} %copy.88.qstart_ref, bf16[512,4096]{1,0:T(8,128)(2,1)} %get-tuple-element.321.q_ref, bf16[3072,512]{1,0:T(8,128)(2,1)} %get-tuple-element.322.k_ref.v_ref, ...), custom_call_target="tpu_custom_call" | custom-call | flops 4294967296 | bytes 2097152 | tf_op jit(solution)/shard_map/cond/branch_1_fun/prefill_attend/pallas_call | solution.py:87
  162.1 0.8 slice.140
  162.9 1.3 select_dynamic-update-slice_fusion.11
  164.2 1.3 select_dynamic-update-slice_fusion.10
  165.6 1.2 select_dynamic-update-slice_fusion.9
  166.8 0.1 select_dynamic-update-slice_fusion.8
  166.9 1.3 select_dynamic-update-slice_fusion.7
  168.4 0.8 copy-done.16
  169.3 57.7 %conditional.5 = (bf16[512,2048]{1,0:T(8,128)(2,1)}, bf16[4,2048]{1,0:T(4,128)(2,1)S(1)}) conditional(s32[]{:T(128)} %convert_element_type.53, (f32[4,4,128]{2,1,0:T(4,128)S(1)}, bf16[512,4096]{1,0:T(8,128)(2,1)S(1)}, bf16[512,512]{1,0:T(8,128)(2,1)S(1)}, bf16[512,512]{1,0:T(8,128)(2,1)S(1)}, bf16[128,16,512]{2,1,0:T(8,128)(2,1)S(1)}, ...), branch_computations={%region_4.5_spmd, %region_5.6_spmd} | conditional | flops 8589934592 | bytes 33591368 | solution.py:377
  169.3 1.7 copy-done.7
  170.9 1.3 copy-done.18
  172.4 53.8 %prefill_attend.3 = bf16[512,2048]{1,0:T(8,128)(2,1)} custom-call(s32[16]{0:T(128)S(1)} %get-tuple-element.283.bounds_ref, s32[512,1]{1,0:T(8,128)S(1)} %get-tuple-element.284.qpos_ref, s32[512,1]{1,0:T(8,128)S(1)} %copy.84.qstart_ref, bf16[512,4096]{1,0:T(8,128)(2,1)} %copy-done.18, bf16[3072,512]{1,0:T(8,128)(2,1)} %copy-done.7, bf16[3072,512]{1,0:T(8,128)(2,1)} %copy-done.7), custom_call_target="tpu_custom_call" | custom-call | flops 8589934592 | bytes 4194304 | tf_op jit(solution)/shard_map/cond/branch_1_fun/prefill_attend/pallas_call | solution.py:87
  226.2 0.8 slice.129
  226.9 0.6 select_dynamic-update-slice_fusion.13.refs_0_
  227.6 10.7 %project.7 = bf16[256,2560]{1,0:T(8,128)(2,1)S(1)} custom-call(s32[1]{0:T(128)} %bitcast.32.base_ref, bf16[512,2048]{1,0:T(8,128)(2,1)} %select_dynamic-update-slice_fusion.13.refs_0_, bf16[256,2048]{1,0:T(8,128)(2,1)S(1)} %get-tuple-element.553.refs_1_, bf16[4096,5120]{1,0:T(8,128)(2,1)} %refs_2_.7), custom_call_target="tpu_custom_call" | custom-call | flops 5368709120 | bytes 20971520 | tf_op jit(solution)/shard_map/project/pallas_call | solution.py:200
  238.3 0.4 collective-permute-start.20
  238.7 0.6 select_dynamic-update-slice_fusion.12.refs_1_
  239.3 11.1 %project.5 = bf16[256,2560]{1,0:T(8,128)(2,1)S(1)} custom-call(s32[1]{0:T(128)} %bitcast.32.base_ref, bf16[512,2048]{1,0:T(8,128)(2,1)} %select_dynamic-update-slice_fusion.13.refs_0_, bf16[256,2048]{1,0:T(8,128)(2,1)} %select_dynamic-update-slice_fusion.12.refs_1_, bf16[4096,5120]{1,0:T(8,128)(2,1)} %refs_2_.7), custom_call_target="tpu_custom_call" | custom-call | flops 5368709120 | bytes 20971520 | tf_op jit(solution)/shard_map/project/pallas_call | solution.py:200
  250.3 1.3 collective-permute-start.19
  251.6 10.8 %project.6 = bf16[256,2560]{1,0:T(8,128)(2,1)S(1)} custom-call(s32[1]{0:T(128)} %bitcast.24.base_ref, bf16[512,2048]{1,0:T(8,128)(2,1)} %select_dynamic-update-slice_fusion.13.refs_0_, bf16[256,2048]{1,0:T(8,128)(2,1)S(1)} %get-tuple-element.553.refs_1_, bf16[4096,5120]{1,0:T(8,128)(2,1)} %refs_2_.7), custom_call_target="tpu_custom_call" | custom-call | flops 5368709120 | bytes 20971520 | tf_op jit(solution)/shard_map/project/pallas_call | solution.py:200
  262.4 11.1 %project.4 = bf16[256,2560]{1,0:T(8,128)(2,1)S(1)} custom-call(s32[1]{0:T(128)} %bitcast.24.base_ref, bf16[512,2048]{1,0:T(8,128)(2,1)} %select_dynamic-update-slice_fusion.13.refs_0_, bf16[256,2048]{1,0:T(8,128)(2,1)} %select_dynamic-update-slice_fusion.12.refs_1_, bf16[4096,5120]{1,0:T(8,128)(2,1)} %refs_2_.7), custom_call_target="tpu_custom_call" | custom-call | flops 5368709120 | bytes 20971520 | tf_op jit(solution)/shard_map/project/pallas_call | solution.py:200
  273.6 0.3 add_convert_fusion
  273.9 0.3 add_convert_fusion.1
  274.2 1.7 pad_maximum_fusion.2
  (80 shorter events, 2.1 us)
Async XLA Ops:
  0.0 13.9 %copy-start.14 = (s32[128]{0:T(128)S(1)}, s32[128]{0:T(128)}, u32[]{:S(2)}) copy-start(s32[128]{0:T(128)} %param.24) | copy-start | bytes 1540
  0.0 14.3 %copy-start.25 = (s32[4]{0:T(128)S(1)}, s32[4]{0:T(128)}, u32[]{:S(2)}) copy-start(s32[4]{0:T(128)} %param.25) | copy-start | bytes 52
  0.0 59.9 %copy-start.20 = (s32[4]{0:T(128)S(1)}, s32[4]{0:T(128)}, u32[]{:S(2)}) copy-start(s32[4]{0:T(128)} %param.26) | copy-start | bytes 52
  2.1 75.7 %collective-permute-start = (bf16[512,512]{1,0:T(8,128)(2,1)}, bf16[512,512]{1,0:T(8,128)(2,1)}, u32[]{:S(2)}, u32[]{:S(2)}) collective-permute-start(bf16[512,512]{1,0:T(8,128)(2,1)} %pad_maximum_fusion.3), channel_id=1, source_target_pairs={{0,4},{1,5},{2,6},{3,7},{8,12},{9,13},{10,14},{11,15}} | collective-permute-start | bytes 1572872 | tf_op jit(solution)/shard_map/ppermute | solution.py:243
  7.2 52.7 %collective-permute-start.5 = (bf16[512,512]{1,0:T(8,128)(2,1)}, bf16[512,512]{1,0:T(8,128)(2,1)S(1)}, u32[]{:S(2)}, u32[]{:S(2)}) collective-permute-start(bf16[512,512]{1,0:T(8,128)(2,1)} %pad_maximum_fusion.3), channel_id=1, source_target_pairs={{0,16},{1,17},{2,18},{3,19},{4,20},{5,21},{6,22},{7,23},{8,24},{9,... | collective-permute-start | bytes 1572872 | tf_op jit(solution)/shard_map/ppermute | solution.py:249
  9.3 50.6 %collective-permute-start.6 = (bf16[512,512]{1,0:T(8,128)(2,1)}, bf16[512,512]{1,0:T(8,128)(2,1)S(1)}, u32[]{:S(2)}, u32[]{:S(2)}) collective-permute-start(bf16[512,512]{1,0:T(8,128)(2,1)} %pad_maximum_fusion.4), channel_id=1, source_target_pairs={{0,16},{1,17},{2,18},{3,19},{4,20},{5,21},{6,22},{7,23},{8,24},{9,... | collective-permute-start | bytes 1572872 | tf_op jit(solution)/shard_map/ppermute | solution.py:249
  10.6 52.5 %collective-permute-start.14 = (bf16[512,512]{1,0:T(8,128)(2,1)}, bf16[512,512]{1,0:T(8,128)(2,1)}, u32[]{:S(2)}, u32[]{:S(2)}) collective-permute-start(bf16[512,512]{1,0:T(8,128)(2,1)} %pad_maximum_fusion.4), channel_id=1, source_target_pairs={{0,4},{1,5},{2,6},{3,7},{8,12},{9,13},{10,14},{11,15}} | collective-permute-start | bytes 1572872 | tf_op jit(solution)/shard_map/ppermute | solution.py:243
  60.3 7.3 %collective-permute-start.7 = (f32[4,4160]{1,0:T(4,128)S(1)}, f32[4,4160]{1,0:T(4,128)S(1)}, u32[]{:S(2)}, u32[]{:S(2)}) collective-permute-start(f32[4,4160]{1,0:T(4,128)S(1)} %bitcast.164), channel_id=1, source_target_pairs={{16,17},{17,18},{18,19},{19,20},{20,21},{21,22},{22,23},{23,16},{2... | collective-permute-start | bytes 199688 | tf_op jit(solution)/shard_map/ppermute | solution.py:307
  61.0 8.5 %collective-permute-start.8 = (f32[4,4160]{1,0:T(4,128)S(1)}, f32[4,4160]{1,0:T(4,128)S(1)}, u32[]{:S(2)}, u32[]{:S(2)}) collective-permute-start(f32[4,4160]{1,0:T(4,128)S(1)} %bitcast.163), channel_id=1, source_target_pairs={{16,18},{17,19},{18,20},{19,21},{20,22},{21,23},{22,16},{23,17},{2... | collective-permute-start | bytes 199688 | tf_op jit(solution)/shard_map/ppermute | solution.py:307
  61.7 8.5 %collective-permute-start.9 = (f32[4,4160]{1,0:T(4,128)S(1)}, f32[4,4160]{1,0:T(4,128)S(1)}, u32[]{:S(2)}, u32[]{:S(2)}) collective-permute-start(f32[4,4160]{1,0:T(4,128)S(1)} %bitcast.162), channel_id=1, source_target_pairs={{16,19},{17,20},{18,21},{19,22},{20,23},{21,16},{22,17},{23,18},{2... | collective-permute-start | bytes 199688 | tf_op jit(solution)/shard_map/ppermute | solution.py:307
  63.2 17.1 %collective-permute-start.2 = (bf16[512,512]{1,0:T(8,128)(2,1)}, bf16[512,512]{1,0:T(8,128)(2,1)S(1)}, u32[]{:S(2)}, u32[]{:S(2)}) collective-permute-start(bf16[512,512]{1,0:T(8,128)(2,1)} %pad_maximum_fusion.3), channel_id=1, source_target_pairs={{0,2},{1,3},{2,4},{3,5},{4,6},{5,7},{8,10},{9,11},{10,12},{11,13},... | collective-permute-start | bytes 1572872 | tf_op jit(solution)/shard_map/ppermute | solution.py:243
  67.6 23.9 %collective-permute-start.16 = (bf16[512,512]{1,0:T(8,128)(2,1)}, bf16[512,512]{1,0:T(8,128)(2,1)S(1)}, u32[]{:S(2)}, u32[]{:S(2)}) collective-permute-start(bf16[512,512]{1,0:T(8,128)(2,1)} %pad_maximum_fusion.4), channel_id=1, source_target_pairs={{0,2},{1,3},{2,4},{3,5},{4,6},{5,7},{8,10},{9,11},{10,12},{11,13},... | collective-permute-start | bytes 1572872 | tf_op jit(solution)/shard_map/ppermute | solution.py:243
  69.6 3.2 %collective-permute-start.10 = (f32[4,4160]{1,0:T(4,128)S(1)}, f32[4,4160]{1,0:T(4,128)S(1)}, u32[]{:S(2)}, u32[]{:S(2)}) collective-permute-start(f32[4,4160]{1,0:T(4,128)S(1)} %bitcast.161), channel_id=1, source_target_pairs={{16,20},{17,21},{18,22},{19,23},{20,16},{21,17},{22,18},{23,19},{2... | collective-permute-start | bytes 199688 | tf_op jit(solution)/shard_map/ppermute | solution.py:307
  70.3 23.8 %collective-permute-start.15 = (bf16[512,512]{1,0:T(8,128)(2,1)}, bf16[512,512]{1,0:T(8,128)(2,1)}, u32[]{:S(2)}, u32[]{:S(2)}) collective-permute-start(bf16[512,512]{1,0:T(8,128)(2,1)} %collective-permute-done.14), channel_id=1, source_target_pairs={{0,1},{1,0},{2,3},{3,2},{4,5},{5,4},{6,7},{7,6},{8,9},{9,8},{10,11... | collective-permute-start | bytes 1572872 | tf_op jit(solution)/shard_map/ppermute | solution.py:246
  72.8 0.7 collective-permute-start.11
  73.6 1.5 collective-permute-start.12
  75.1 0.7 collective-permute-start.13
  75.8 91.1 %collective-permute-start.4 = (bf16[512,512]{1,0:T(8,128)(2,1)}, bf16[512,512]{1,0:T(8,128)(2,1)}, u32[]{:S(2)}, u32[]{:S(2)}) collective-permute-start(bf16[512,512]{1,0:T(8,128)(2,1)} %pad_maximum_fusion.3), channel_id=1, source_target_pairs={{0,1},{1,0},{2,3},{3,2},{4,5},{5,4},{6,7},{7,6},{8,9},{9,8},{10,11... | collective-permute-start | bytes 1572872 | tf_op jit(solution)/shard_map/ppermute | solution.py:246
  77.8 21.2 %collective-permute-start.18 = (bf16[512,512]{1,0:T(8,128)(2,1)}, bf16[512,512]{1,0:T(8,128)(2,1)S(1)}, u32[]{:S(2)}, u32[]{:S(2)}) collective-permute-start(bf16[512,512]{1,0:T(8,128)(2,1)} %pad_maximum_fusion.4), channel_id=1, source_target_pairs={{0,1},{1,0},{2,3},{3,2},{4,5},{5,4},{6,7},{7,6},{8,9},{9,8},{10,11... | collective-permute-start | bytes 1572872 | tf_op jit(solution)/shard_map/ppermute | solution.py:246
  80.3 82.6 %collective-permute-start.1 = (bf16[512,512]{1,0:T(8,128)(2,1)}, bf16[512,512]{1,0:T(8,128)(2,1)}, u32[]{:S(2)}, u32[]{:S(2)}) collective-permute-start(bf16[512,512]{1,0:T(8,128)(2,1)} %collective-permute-done), channel_id=1, source_target_pairs={{0,1},{1,0},{2,3},{3,2},{4,5},{5,4},{6,7},{7,6},{8,9},{9,8},{10,11... | collective-permute-start | bytes 1572872 | tf_op jit(solution)/shard_map/ppermute | solution.py:246
  91.5 74.0 %collective-permute-start.3 = (bf16[512,512]{1,0:T(8,128)(2,1)S(1)}, bf16[512,512]{1,0:T(8,128)(2,1)}, u32[]{:S(2)}, u32[]{:S(2)}) collective-permute-start(bf16[512,512]{1,0:T(8,128)(2,1)S(1)} %collective-permute-done.2), channel_id=1, source_target_pairs={{0,1},{1,0},{2,3},{3,2},{4,5},{5,4},{6,7},{7,6},{8,9},{9,8},{10,11... | collective-permute-start | bytes 1572872 | tf_op jit(solution)/shard_map/ppermute | solution.py:246
  94.1 4.6 %collective-permute-start.17 = (bf16[512,512]{1,0:T(8,128)(2,1)S(1)}, bf16[512,512]{1,0:T(8,128)(2,1)S(1)}, u32[]{:S(2)}, u32[]{:S(2)}) collective-permute-start(bf16[512,512]{1,0:T(8,128)(2,1)S(1)} %collective-permute-done.16), channel_id=1, source_target_pairs={{0,1},{1,0},{2,3},{3,2},{4,5},{5,4},{6,7},{7,6},{8,9},{9,8},{10,11... | collective-permute-start | bytes 1572872 | tf_op jit(solution)/shard_map/ppermute | solution.py:246
  96.0 3.3 %copy-start.23 = (bf16[128,16,512]{2,1,0:T(8,128)(2,1)S(1)}, bf16[128,16,512]{2,1,0:T(8,128)(2,1)}, u32[]{:S(2)}) copy-start(bf16[128,16,512]{2,1,0:T(8,128)(2,1)} %param.23) | copy-start | bytes 6291460
  97.4 2.0 copy-start.21
  98.7 3.4 %copy-start.15 = (bf16[512,4096]{1,0:T(8,128)(2,1)S(1)}, bf16[512,4096]{1,0:T(8,128)(2,1)}, u32[]{:S(2)}) copy-start(bf16[512,4096]{1,0:T(8,128)(2,1)} %param.19) | copy-start | bytes 12582916
  98.9 3.3 %copy-start.1 = (bf16[512,512]{1,0:T(8,128)(2,1)S(1)}, bf16[512,512]{1,0:T(8,128)(2,1)}, u32[]{:S(2)}) copy-start(bf16[512,512]{1,0:T(8,128)(2,1)} %param.20) | copy-start | bytes 1572868
  98.9 3.4 %copy-start.2 = (bf16[512,512]{1,0:T(8,128)(2,1)S(1)}, bf16[512,512]{1,0:T(8,128)(2,1)}, u32[]{:S(2)}) copy-start(bf16[512,512]{1,0:T(8,128)(2,1)} %param.21) | copy-start | bytes 1572868
  98.9 3.4 %copy-start.19 = (s32[16]{0:T(128)S(1)}, s32[16]{0:T(128)}, u32[]{:S(2)}) copy-start(s32[16]{0:T(128)} %reshape.391) | copy-start | bytes 196
  99.3 3.0 %copy-start.5 = (bf16[3072,512]{1,0:T(8,128)(2,1)}, bf16[3072,512]{1,0:T(8,128)(2,1)S(1)}, u32[]{:S(2)}) copy-start(bf16[3072,512]{1,0:T(8,128)(2,1)S(1)} %select_dynamic-update-slice_fusion) | copy-start | bytes 9437188
  102.4 1.8 copy-start.6
  102.4 3.0 %copy-start.17 = (bf16[512,4096]{1,0:T(8,128)(2,1)}, bf16[512,4096]{1,0:T(8,128)(2,1)S(1)}, u32[]{:S(2)}) copy-start(bf16[512,4096]{1,0:T(8,128)(2,1)S(1)} %get-tuple-element.332.q_ref) | copy-start | bytes 12582916 | tf_op jit(solution)/shard_map/cond
  162.8 5.6 %copy-start.24 = (bf16[128,16,512]{2,1,0:T(8,128)(2,1)S(1)}, bf16[128,16,512]{2,1,0:T(8,128)(2,1)}, u32[]{:S(2)}) copy-start(bf16[128,16,512]{2,1,0:T(8,128)(2,1)} %param.23) | copy-start | bytes 6291460
  164.2 4.2 %copy-start.22 = (bf16[128,16,512]{2,1,0:T(8,128)(2,1)S(1)}, bf16[128,16,512]{2,1,0:T(8,128)(2,1)}, u32[]{:S(2)}) copy-start(bf16[128,16,512]{2,1,0:T(8,128)(2,1)} %param.22) | copy-start | bytes 6291460
  166.7 1.7 copy-start.3
  166.8 2.5 copy-start.16
  169.3 1.7 copy-start.7
  169.3 2.9 %copy-start.18 = (bf16[512,4096]{1,0:T(8,128)(2,1)}, bf16[512,4096]{1,0:T(8,128)(2,1)S(1)}, u32[]{:S(2)}) copy-start(bf16[512,4096]{1,0:T(8,128)(2,1)S(1)} %get-tuple-element.286.q_ref) | copy-start | bytes 12582916 | tf_op jit(solution)/shard_map/cond
  238.3 35.3 %collective-permute-start.20 = (bf16[256,2560]{1,0:T(8,128)(2,1)S(1)}, bf16[256,2560]{1,0:T(8,128)(2,1)S(1)}, u32[]{:S(2)}, u32[]{:S(2)}) collective-permute-start(bf16[256,2560]{1,0:T(8,128)(2,1)S(1)} %project.7), channel_id=1, source_target_pairs={{0,8},{8,0},{1,9},{9,1},{2,10},{10,2},{3,11},{11,3},{4,12},{12,4},... | collective-permute-start | bytes 3932168 | tf_op jit(solution)/shard_map/ppermute | solution.py:406
  250.3 23.6 %collective-permute-start.19 = (bf16[256,2560]{1,0:T(8,128)(2,1)S(1)}, bf16[256,2560]{1,0:T(8,128)(2,1)S(1)}, u32[]{:S(2)}, u32[]{:S(2)}) collective-permute-start(bf16[256,2560]{1,0:T(8,128)(2,1)S(1)} %project.5), channel_id=1, source_target_pairs={{0,8},{8,0},{1,9},{9,1},{2,10},{10,2},{3,11},{11,3},{4,12},{12,4},... | collective-permute-start | bytes 3932168 | tf_op jit(solution)/shard_map/ppermute | solution.py:406
